TPU v7x, 32 devices: a whole 2x2x4 slice. The times are simulated.
32 devices in a mesh: groups: 2 (over x), yslab: 16 (over z, y, core).
Axes of the slice: x: 2, y: 2, z: 4, core: 2. Of those that a mesh axis runs over, the one named last changes fastest.
Arguments:
- signal: bfloat16 [20, 64, 64, 128], P(None, 'groups', 'yslab'), parts along dimension 1, may hold values from -6 to 6
- cotangent: bfloat16 [20, 64, 64, 128], P(None, 'groups', 'yslab'), parts along dimension 1, may hold values from -6 to 6
- spectral_weight: bfloat16 [512, 25600], P('yslab'), may hold values from -1.25 to 1.25
- mix_weight: float32 [20, 20], replicated, may hold values from -1.25 to 1.25
- mix_bias: float32 [20], replicated, may hold values from -3 to 3
Outputs:
- activation: bfloat16 [20, 64, 64, 128], P(None, 'groups', 'yslab'), parts along dimension 1
- grad_input: bfloat16 [20, 64, 64, 128], P(None, 'groups', 'yslab'), parts along dimension 1
- grad_spectral: float32 [512, 51200], P('yslab', 'groups'), parts along dimension 1
- grad_mix: float32 [40, 20], P('groups'), parts along dimension 0
- grad_bias: float32 [40], P('groups'), parts along dimension 0
There are 2 independent parts, one for each index of `groups`. A program takes and returns all parts, laid end to end along the dimension named above; an argument that names none is the same for every part. Nothing has to cross between parts.
All inputs are finite; a program needn't handle non-finite values.
Results may differ from a plain program's by a relative error of at most 0.001.
Values sent between devices are 32-bit elements; how exact they have to be, the bound alone decides.
A program may use at most 128 MiB of HBM per device.

v0:
```python
from functools import partial
import math

import ml_dtypes
import numpy as np

import jax
import jax.numpy as jnp
from jax import lax
from jax.experimental import pallas as pl
from jax.experimental.pallas import tpu as pltpu
from jax.sharding import PartitionSpec as P

MODES = 16
PAIRS = 512


def contract(form, left, right):
    return jnp.einsum(
        form, left, right, precision=lax.Precision.HIGH, preferred_element_type=jnp.float32
    )


def signed_waves(modes):
    return jnp.concatenate(
        [jnp.arange(modes, dtype=jnp.int32), jnp.arange(-modes, 0, dtype=jnp.int32)]
    )


def tables(places, length, wavenum):
    phase = jnp.mod(places[:, None] * wavenum[None, :], length).astype(jnp.float32)
    angle = phase * (2.0 * math.pi / length)
    return (jnp.cos(angle), jnp.sin(angle))


def per_device_general(signal, cotangent, spectral_weight, mix_weight, mix_bias):
    channels, width_x, rows_y, width_z = signal.shape
    slabs = lax.axis_size("yslab")
    length_y = rows_y * slabs
    waves = signed_waves(MODES)
    cos_x, sin_x = tables(jnp.arange(width_x, dtype=jnp.int32), width_x, waves)
    cos_z, sin_z = tables(
        jnp.arange(width_z, dtype=jnp.int32), width_z, jnp.arange(MODES, dtype=jnp.int32)
    )
    scale_fwd = 1.0 / math.sqrt(width_x * length_y * width_z)
    scale_inv = 1.0 / math.sqrt(4 * MODES**3)

    all_rows = jnp.arange(length_y, dtype=jnp.int32)
    cos_y, sin_y = tables(all_rows, length_y, waves)
    turn_y = jnp.stack(
        [jnp.stack([cos_y, -sin_y], axis=1), jnp.stack([sin_y, cos_y], axis=1)]
    ).reshape(2, slabs, rows_y, 2, 2 * MODES)
    owned = PAIRS // slabs
    back_x = jnp.stack([jnp.stack([cos_x, sin_x]), jnp.stack([-sin_x, cos_x])])
    turn_z = jnp.stack([cos_z, -sin_z])

    def to_modes(field, scale):
        first = contract("cxyz,rzk->rcxyk", field, turn_z)
        second = contract(
            "rcxyk,rqxj->qcyjk", first, jnp.stack(
                [jnp.stack([cos_x, -sin_x]), jnp.stack([sin_x, cos_x])]
            )
        )
        blocks = second.reshape(2, channels, rows_y, slabs, owned)
        blocks = jnp.transpose(blocks, (3, 0, 2, 1, 4))
        rows = lax.all_to_all(blocks, "yslab", split_axis=0, concat_axis=0, tiled=True)
        return contract("sqycp,qsyrm->prcm", rows, turn_y) * scale

    def to_grid(spectrum, scale):
        rows = contract("prcm,rsyqm->sqycp", spectrum, jnp.transpose(turn_y, (3, 1, 2, 0, 4)))
        rows = lax.all_to_all(rows, "yslab", split_axis=0, concat_axis=0, tiled=True)
        shaped = jnp.transpose(rows, (1, 3, 2, 0, 4)).reshape(
            2, channels, rows_y, 2 * MODES, MODES
        )
        second = contract("qcyjk,qrxj->rcxyk", shaped, back_x)
        return contract("rcxyk,rzk->cxyz", second, turn_z) * scale

    weights = spectral_weight.astype(jnp.float32).reshape(-1, 2, channels, channels, 2 * MODES)
    w_real = weights[:, 0]
    w_imag = weights[:, 1]
    spectrum = to_modes(signal, scale_fwd)
    modes_re = spectrum[:, 0]
    modes_im = spectrum[:, 1]
    mixed_re = contract("pcom,pcm->pom", w_real, modes_re) - contract(
        "pcom,pcm->pom", w_imag, modes_im
    )
    mixed_im = contract("pcom,pcm->pom", w_real, modes_im) + contract(
        "pcom,pcm->pom", w_imag, modes_re
    )
    spectral = to_grid(jnp.stack([mixed_re, mixed_im], axis=1), scale_inv)
    pre = spectral + contract("cxyz,co->oxyz", signal, mix_weight) + mix_bias[:, None, None, None]
    result, pullback = jax.vjp(partial(jax.nn.gelu, approximate=True), pre)
    activation = result.astype(jnp.bfloat16)
    dpre = pullback(cotangent.astype(jnp.float32))[0]
    dmixed = to_modes(dpre, scale_inv)
    dmixed_re = dmixed[:, 0]
    dmixed_im = dmixed[:, 1]
    dweight_re = contract("pcm,pom->pcom", modes_re, dmixed_re) + contract(
        "pcm,pom->pcom", modes_im, dmixed_im
    )
    dweight_im = contract("pcm,pom->pcom", modes_re, dmixed_im) - contract(
        "pcm,pom->pcom", modes_im, dmixed_re
    )
    grad_spectral = jnp.stack([dweight_re, dweight_im], axis=1).reshape(
        spectral_weight.shape[0], -1
    )
    dmodes_re = contract("pcom,pom->pcm", w_real, dmixed_re) + contract(
        "pcom,pom->pcm", w_imag, dmixed_im
    )
    dmodes_im = contract("pcom,pom->pcm", w_real, dmixed_im) - contract(
        "pcom,pom->pcm", w_imag, dmixed_re
    )
    back_field = to_grid(jnp.stack([dmodes_re, dmodes_im], axis=1), scale_fwd)
    grad_input = (back_field + contract("oxyz,co->cxyz", dpre, mix_weight)).astype(jnp.bfloat16)
    mix_sum, bias_sum = lax.psum(
        (contract("cxyz,oxyz->co", signal, dpre), jnp.sum(dpre, axis=(1, 2, 3))), "yslab"
    )
    return (activation, grad_input, grad_spectral, mix_sum * scale_fwd, bias_sum * scale_fwd)


SLABS = 16
ROWS = 4
F32 = jnp.float32
BF16 = jnp.bfloat16
CHANS = [[oq * 4 + 2 * q + ii for ii in range(2) for oq in range(4)] for q in range(2)]
CHANS.append([16, 17, 18, 19])
CHUNKS = [(0, 2), (2, 2), (4, 1)]


def split_table(table):
    high = table.astype(ml_dtypes.bfloat16)
    low = (table - high.astype(np.float64)).astype(ml_dtypes.bfloat16)
    return np.stack([high, low])


def host_waves(places, length, wavenum):
    angle = np.mod(np.outer(places, wavenum), length) * (2.0 * math.pi / length)
    return np.cos(angle), np.sin(angle)


def host_tables(width_x, length_y, width_z):
    waves = np.concatenate([np.arange(MODES), np.arange(-MODES, 0)])
    cx, sx = host_waves(np.arange(width_x), width_x, waves)
    cy, sy = host_waves(np.arange(length_y), length_y, waves)
    cz, sz = host_waves(np.arange(width_z), width_z, np.arange(MODES))
    eye_y = np.eye(ROWS)
    fz = np.stack([cz, -sz])
    z8 = np.einsum("ab,rzk->azrbk", np.eye(8), fz).reshape(8 * width_z, 256)
    z4 = np.einsum("ab,rzk,e->azrebk", np.eye(4), fz, np.ones(2)).reshape(4 * width_z, 256)
    fx = np.stack([np.stack([cx, -sx]), np.stack([sx, cx])])
    wx = np.einsum("rqxdl,yt->ldyqrxt", fx.reshape(2, 2, width_x, SLABS, 2), eye_y)
    wx = wx.reshape(256, 256)
    bx = np.stack([np.stack([cx, sx]), np.stack([-sx, cx])])
    wxi = np.einsum("qrxdl,yt->rxtldyq", bx.reshape(2, 2, width_x, SLABS, 2), eye_y)
    wxi = wxi.reshape(256, 256)
    fy = np.stack([np.stack([cy, -sy]), np.stack([sy, cy])])
    ty = np.einsum("rqym,e->yrqem", fy, np.ones(4)).reshape(128, 256)
    by = np.stack([np.stack([cy, sy]), np.stack([-sy, cy])])
    tyi = np.einsum("rqym,ie->iyqrem", by, np.eye(4)).reshape(512, 256)
    tyr = np.einsum("rqym,e->yqrem", by, np.ones(4)).reshape(128, 256)
    zi8 = np.einsum("ab,rzk->rakbz", np.eye(8), fz).reshape(256, 8 * width_z)
    pick = np.stack([np.ones(1), np.zeros(1)]).reshape(2)
    zi4 = np.einsum("ab,rzk,e->raekbz", np.eye(4), fz, pick).reshape(256, 4 * width_z)
    return [split_table(t) for t in (z8, z4, wx, wxi, ty, tyi, tyr, zi8, zi4)]


def halves(value):
    high = value.astype(BF16)
    return high, (value - high.astype(F32)).astype(BF16)


def product(left, right, form=((1,), (0,))):
    def one(a, b):
        return lax.dot_general(a, b, (form, ((), ())), preferred_element_type=F32)

    total = one(left[0], right[0])
    if left[1] is not None:
        total = total + one(left[1], right[0])
    if right[1] is not None:
        total = total + one(left[0], right[1])
    return total


def block_kernel(scale_fwd, scale_inv, sig, cot, w, mix, bias, z8, z4, wx, wxi, ty, tyi, tyr, zi8,
                 zi4, act, gin, gspec, gsum, sf, point, dpre, modes, dmodes, spec, dspec, gmix,
                 send, recv, sums, send_sem, recv_sem, sum_send, sum_recv):
    me = lax.axis_index("yslab")
    channels = 20
    lane = lax.broadcasted_iota(jnp.int32, (128, 128), 1)

    def both(ref):
        return ref[0], ref[1]

    def copy(step, chunk, peer):
        first, count = CHUNKS[chunk]
        return pltpu.make_async_remote_copy(
            src_ref=send.at[step, peer, pl.ds(first, count)],
            dst_ref=recv.at[step, me, pl.ds(first, count)],
            send_sem=send_sem.at[step, chunk, peer],
            recv_sem=recv_sem.at[step, chunk, me],
            device_id={"yslab": peer},
            device_id_type=pl.DeviceIdType.MESH,
        )

    def arrival(step, chunk, peer):
        first, count = CHUNKS[chunk]
        return pltpu.make_async_remote_copy(
            src_ref=send.at[step, peer, pl.ds(first, count)],
            dst_ref=recv.at[step, peer, pl.ds(first, count)],
            send_sem=send_sem.at[step, chunk, peer],
            recv_sem=recv_sem.at[step, chunk, peer],
            device_id={"yslab": peer},
            device_id_type=pl.DeviceIdType.MESH,
        )

    def sum_copy(peer, source):
        return pltpu.make_async_remote_copy(
            src_ref=sums.at[me],
            dst_ref=sums.at[source],
            send_sem=sum_send.at[peer],
            recv_sem=sum_recv.at[source],
            device_id={"yslab": peer},
            device_id_type=pl.DeviceIdType.MESH,
        )

    def each_peer(action):
        def body(i, carry):
            action(lax.rem(me + i, SLABS))
            return carry

        lax.fori_loop(1, SLABS, body, 0)

    def send_chunk(step, chunk):
        each_peer(lambda peer: copy(step, chunk, peer).start())
        first, count = CHUNKS[chunk]
        recv[step, pl.ds(me, 1), first:first + count] = send[step, pl.ds(me, 1), first:first + count]

    def wait_chunk(step, chunk):
        each_peer(lambda peer: arrival(step, chunk, peer).wait_recv())

    def forward_group(step, group, read, exact):
        table = z8 if group < 2 else z4
        total = None
        for at in range(0, len(CHANS[group]), 2):
            pair = jnp.concatenate([read(c) for c in CHANS[group][at:at + 2]], axis=1)
            left = (pair, None) if exact else halves(pair)
            rows = slice(at * 128, at * 128 + 256)
            part = product(left, (table[0, rows], table[1, rows]))
            total = part if total is None else total + part
        stacked = jnp.concatenate([total[:, :128], total[:, 128:]], axis=0)
        out = product(both(wx), halves(stacked))
        if group < 2:
            for jl in range(2):
                send[step, :, 2 * group + jl] = out[jl * 128:(jl + 1) * 128].reshape(16, 8, 128)
        else:
            send[step, :, 4] = jnp.where(lane < 64, out[:128], out[128:]).reshape(16, 8, 128)
        send_chunk(step, group)

    def spectra(step, group, target, scale):
        for jl in range(2 if group < 2 else 1):
            tile = recv[step, :, 2 * group + jl].reshape(128, 128) * scale
            out = product(halves(tile.T), both(ty))
            if group < 2:
                for place, c in enumerate(CHANS[group]):
                    target[jl, c] = out[place * 16:(place + 1) * 16]
            else:
                for jj in range(2):
                    for place, c in enumerate(CHANS[2]):
                        row = jj * 64 + place * 16
                        target[jj, c] = out[row:row + 16]

    def back_group(step, group, use):
        if group < 2:
            one = recv[step, :, 2 * group].reshape(128, 128)
            two = recv[step, :, 2 * group + 1].reshape(128, 128)
            top = jnp.where(lane < 64, one, pltpu.roll(two, 64, 1))
            low = jnp.where(lane < 64, pltpu.roll(one, 64, 1), two)
        else:
            top = recv[step, :, 4].reshape(128, 128)
            low = pltpu.roll(top, 112, 1)
        out = product(both(wxi), halves(jnp.concatenate([top, low], axis=0)))
        left = halves(jnp.concatenate([out[:128], out[128:]], axis=1))
        table = zi8 if group < 2 else zi4
        for at in range(0, len(CHANS[group]), 2):
            cols = slice(at * 128, at * 128 + 256)
            field = product(left, (table[0, :, cols], table[1, :, cols]))
            use(CHANS[group][at], field[:, :128])
            use(CHANS[group][at + 1], field[:, 128:])

    def pointwise(source, weight, start):
        def block(at, carry):
            rows = pl.ds(pl.multiple_of(lax.rem(at, 4) * 32, 32), 32)
            first = lax.div(at, 4) * 4
            totals = [jnp.full((32, 128), start(first + i), F32) for i in range(4)]
            for b in range(channels):
                value = source[b, rows]
                for i in range(4):
                    totals[i] = totals[i] + weight(first + i, b) * value
            for i in range(4):
                point[first + i, rows] = totals[i]
            return carry

        lax.fori_loop(0, 20, block, 0)

    barrier = pltpu.get_barrier_semaphore()

    def greet(peer):
        pl.semaphore_signal(barrier, inc=1, device_id={"yslab": peer},
                            device_id_type=pl.DeviceIdType.MESH)

    each_peer(greet)
    pl.semaphore_wait(barrier, SLABS - 1)

    for group in range(3):
        forward_group(0, group, lambda c: sig[c], True)
    sf[...] = sig[...].astype(F32)
    pointwise(sf, lambda a, b: mix[b, a], lambda a: bias[a])
    for group in range(3):
        wait_chunk(0, group)
        spectra(0, group, modes, scale_fwd)

    for jl in range(2):
        rows = slice(jl * 16, jl * 16 + 16)

        def add(c, total):
            real, imag = total
            wr = w[rows, pl.ds(pl.multiple_of(c * 640, 128), 640)].astype(F32)
            wi = w[rows, pl.ds(pl.multiple_of(c * 640 + 12800, 128), 640)].astype(F32)
            value = modes[jl, c]
            ur = jnp.concatenate([value[:, :128]] * 5, axis=1)
            ui = jnp.concatenate([value[:, 128:]] * 5, axis=1)
            return real + wr * ur - wi * ui, imag + wr * ui + wi * ur

        zero = jnp.zeros((16, 640), F32)
        real, imag = lax.fori_loop(0, channels, add, (zero, zero))
        for oq in range(5):
            cols = slice(oq * 128, (oq + 1) * 128)
            if oq < 4:
                starts = [jl * 64 + oq * 16]
            else:
                starts = [128 + dup * 32 + jl * 16 for dup in range(4)]
            for row in starts:
                spec[row:row + 16, :128] = real[:, cols]
                spec[row:row + 16, 128:] = imag[:, cols]
    grid = product(both(tyi), halves(spec[...] * scale_inv), ((1,), (1,)))
    last = jnp.zeros((128, 128), F32)
    for i in range(4):
        send[1, :, i] = grid[i * 128:(i + 1) * 128, :128].reshape(16, 8, 128)
        last = jnp.where(lane // 32 == i, grid[i * 128:(i + 1) * 128, 128:], last)
    send[1, :, 4] = last.reshape(16, 8, 128)
    for group in range(3):
        send_chunk(1, group)

    def activate(o, field):
        value = field + point[o]
        root = math.sqrt(2.0 / math.pi)
        square = value * value
        t = jnp.tanh(root * value * (1.0 + 0.044715 * square))
        half = 0.5 * (1.0 + t)
        act[o] = (value * half).astype(BF16)
        slope = half + 0.5 * value * (1.0 - t * t) * root * (1.0 + 3 * 0.044715 * square)
        dpre[o] = cot[o].astype(F32) * slope

    for group in range(3):
        wait_chunk(1, group)
        back_group(1, group, activate)
        forward_group(2, group, lambda c: dpre[c], False)

    pointwise(dpre, lambda a, b: mix[a, b], lambda a: 0.0)

    def reduce_rows(value):
        return jnp.sum(value, axis=0, keepdims=True)

    def pair_sums(c, carry):
        field = sf[c]
        for o in range(channels):
            gmix[c, o:o + 1] = reduce_rows(field * dpre[o])
        return carry

    gmix[...] = jnp.zeros_like(gmix)
    lax.fori_loop(0, channels, pair_sums, 0)
    for o in range(channels):
        gmix[channels, o:o + 1] = reduce_rows(dpre[o])
    flat = jnp.concatenate([gmix[...].reshape(504, 128), jnp.zeros((8, 128), F32)], axis=0)
    line = lax.broadcasted_iota(jnp.int32, (8, 128), 0)
    ones = jnp.ones((8, 128), BF16)
    packed = jnp.zeros((8, 128), F32)
    for r in range(4):
        high, low = halves(flat[r * 128:(r + 1) * 128])
        value = product((ones, None), (high, low), ((1,), (1,)))
        packed = jnp.where(line == r, value, packed)
    sums[pl.ds(me, 1)] = (packed * scale_fwd).reshape(1, 8, 128)
    each_peer(lambda peer: sum_copy(peer, me).start())

    for group in range(3):
        wait_chunk(2, group)
        spectra(2, group, dmodes, scale_inv)

    lanes = lax.broadcasted_iota(jnp.int32, (16, 128), 1) // 32
    for jl in range(2):
        rows = slice(jl * 16, jl * 16 + 16)
        parts = []
        for ri in range(2):
            tiles = []
            for oq in range(5):
                tile = dmodes[jl, oq * 4, :, ri * 128:ri * 128 + 128]
                for i in range(1, 4):
                    other = dmodes[jl, oq * 4 + i, :, ri * 128:ri * 128 + 128]
                    tile = jnp.where(lanes == i, other, tile)
                tiles.append(tile)
            parts.append(jnp.concatenate(tiles, axis=1))
        dr, di = parts

        for c in range(channels):
            wr = w[rows, c * 640:c * 640 + 640].astype(F32)
            wi = w[rows, c * 640 + 12800:c * 640 + 13440].astype(F32)
            real = wr * dr + wi * di
            imag = wr * di - wi * dr
            if c < 16:
                row = (c % 4) * 128 + jl * 64 + (c // 4) * 16
            else:
                row = 512 + (c - 16) * 32 + jl * 16
            for ri, value in ((0, real), (1, imag)):
                folded = value[:, :128]
                for oq in range(1, 5):
                    folded = folded + value[:, oq * 128:(oq + 1) * 128]
                dspec[row:row + 16, ri * 128:ri * 128 + 128] = folded
    for t in range(5):
        grid = product(both(tyr), halves(dspec[t * 128:(t + 1) * 128] * scale_fwd), ((1,), (1,)))
        send[3, :, t] = grid.reshape(16, 8, 128)
        if t == 1 or t == 3 or t == 4:
            send_chunk(3, t // 2)

    for jl in range(2):
        rows = slice(jl * 16, jl * 16 + 16)
        parts = []
        for ri in range(2):
            tiles = []
            for oq in range(5):
                tile = dmodes[jl, oq * 4, :, ri * 128:ri * 128 + 128]
                for i in range(1, 4):
                    other = dmodes[jl, oq * 4 + i, :, ri * 128:ri * 128 + 128]
                    tile = jnp.where(lanes == i, other, tile)
                tiles.append(tile)
            parts.append(jnp.concatenate(tiles, axis=1))
        dr, di = parts

        def outer(c, carry):
            value = modes[jl, c]
            ur = jnp.concatenate([value[:, :128]] * 5, axis=1)
            ui = jnp.concatenate([value[:, 128:]] * 5, axis=1)
            gspec[rows, pl.ds(pl.multiple_of(c * 640, 128), 640)] = ur * dr + ui * di
            gspec[rows, pl.ds(pl.multiple_of(c * 640 + 12800, 128), 640)] = ur * di - ui * dr
            return carry

        lax.fori_loop(0, channels, outer, 0)

    each_peer(lambda peer: sum_copy(peer, peer).wait_recv())
    gsum[...] = jnp.sum(sums[...], axis=0)

    def finish(c, field):
        gin[c] = (field + point[c]).astype(BF16)

    for group in range(3):
        wait_chunk(3, group)
        back_group(3, group, finish)

    each_peer(lambda peer: sum_copy(peer, me).wait_send())
    for step in range(4):
        for group in range(3):
            each_peer(lambda peer: copy(step, group, peer).wait_send())


def per_device(signal, cotangent, spectral_weight, mix_weight, mix_bias):
    channels, width_x, rows_y, width_z = signal.shape
    slabs = lax.axis_size("yslab")
    if (channels, width_x, rows_y, width_z, slabs) != (20, 32, ROWS, 128, SLABS):
        return per_device_general(signal, cotangent, spectral_weight, mix_weight, mix_bias)
    length_y = rows_y * slabs
    scale_fwd = 1.0 / math.sqrt(width_x * length_y * width_z)
    scale_inv = 1.0 / math.sqrt(4 * MODES**3)
    tables_in = [jnp.asarray(t) for t in host_tables(width_x, length_y, width_z)]
    flat = (channels, width_x * rows_y, width_z)
    vmem = pl.BlockSpec(memory_space=pltpu.VMEM)
    smem = pl.BlockSpec(memory_space=pltpu.SMEM)
    act, gin, gspec, gsum = pl.pallas_call(
        partial(block_kernel, scale_fwd, scale_inv),
        out_shape=(
            jax.ShapeDtypeStruct(flat, BF16),
            jax.ShapeDtypeStruct(flat, BF16),
            jax.ShapeDtypeStruct(spectral_weight.shape, F32),
            jax.ShapeDtypeStruct((8, 128), F32),
        ),
        in_specs=[vmem, vmem, vmem, smem, smem] + [vmem] * len(tables_in),
        out_specs=(vmem, vmem, vmem, vmem),
        scratch_shapes=[
            pltpu.VMEM(flat, F32),
            pltpu.VMEM(flat, F32),
            pltpu.VMEM(flat, F32),
            pltpu.VMEM((2, 20, 16, 256), F32),
            pltpu.VMEM((2, 20, 16, 256), F32),
            pltpu.VMEM((256, 256), F32),
            pltpu.VMEM((640, 256), F32),
            pltpu.VMEM((21, 24, 128), F32),
            pltpu.VMEM((4, SLABS, 5, 8, 128), F32),
            pltpu.VMEM((4, SLABS, 5, 8, 128), F32),
            pltpu.VMEM((SLABS, 8, 128), F32),
            pltpu.SemaphoreType.DMA((4, 3, SLABS)),
            pltpu.SemaphoreType.DMA((4, 3, SLABS)),
            pltpu.SemaphoreType.DMA((SLABS,)),
            pltpu.SemaphoreType.DMA((SLABS,)),
        ],
        compiler_params=pltpu.CompilerParams(
            collective_id=0, has_side_effects=True, vmem_limit_bytes=48 * 1024 * 1024
        ),
    )(
        signal.reshape(flat), cotangent.reshape(flat), spectral_weight, mix_weight, mix_bias,
        *tables_in,
    )
    full = gsum[:4].reshape(512)[:504].reshape(21, 24)
    return (
        act.reshape(signal.shape), gin.reshape(signal.shape), gspec, full[:20, :20], full[20, :20],
    )


def solution(mesh):
    placed = (
        P(None, "groups", "yslab", None),
        P(None, "groups", "yslab", None),
        P("yslab", None),
        P(),
        P(),
    )
    return jax.shard_map(
        per_device,
        mesh=mesh,
        in_specs=placed,
        out_specs=(
            P(None, "groups", "yslab", None),
            P(None, "groups", "yslab", None),
            P("yslab", "groups"),
            P("groups", None),
            P("groups"),
        ),
        check_vma=False,
    )
```

profile of v0, /device:TPU:0, one launch (start us, length us, event | category | flops | bytes accessed | tf_op | source)
XLA Modules:
  0.0 73.0 jit_solution(3845252750437583259)
XLA Ops:
  0.6 0.0 copy-start
  0.6 1.2 %copy-done = bf16[2,1024,256]{2,1,0:T(8,128)(2,1)S(1)} copy-done((bf16[2,1024,256]{2,1,0:T(8,128)(2,1)S(1)}, bf16[2,1024,256]{2,1,0:T(8,128)(2,1)}, u32[]{:S(2)}) %copy-start) | copy-done | bytes 1048600
  1.9 0.0 copy-start.1
  1.9 1.1 %copy-done.1 = bf16[20,32,4,128]{3,2,1,0:T(4,128)(2,1)S(1)} copy-done((bf16[20,32,4,128]{3,2,1,0:T(4,128)(2,1)S(1)}, bf16[20,32,4,128]{3,2,1,0:T(4,128)(2,1)}, u32[]{:S(2)}) %copy-start.1) | copy-done | bytes 655384
  2.9 0.0 copy-start.2
  3.0 1.1 %copy-done.2 = bf16[20,32,4,128]{3,2,1,0:T(4,128)(2,1)S(1)} copy-done((bf16[20,32,4,128]{3,2,1,0:T(4,128)(2,1)S(1)}, bf16[20,32,4,128]{3,2,1,0:T(4,128)(2,1)}, u32[]{:S(2)}) %copy-start.2) | copy-done | bytes 655384
  4.0 0.0 copy-start.3
  4.0 0.9 %copy-done.3 = bf16[2,128,256]{2,1,0:T(8,128)(2,1)S(1)} copy-done((bf16[2,128,256]{2,1,0:T(8,128)(2,1)S(1)}, bf16[2,128,256]{2,1,0:T(8,128)(2,1)}, u32[]{:S(2)}) %copy-start.3) | copy-done | bytes 131096
  4.9 0.0 copy-start.4
  4.9 1.0 %copy-done.4 = bf16[2,512,256]{2,1,0:T(8,128)(2,1)S(1)} copy-done((bf16[2,512,256]{2,1,0:T(8,128)(2,1)S(1)}, bf16[2,512,256]{2,1,0:T(8,128)(2,1)}, u32[]{:S(2)}) %copy-start.4) | copy-done | bytes 524312
  6.0 1.0 %copy-done.5 = bf16[2,512,256]{2,1,0:T(8,128)(2,1)S(1)} copy-done((bf16[2,512,256]{2,1,0:T(8,128)(2,1)S(1)}, bf16[2,512,256]{2,1,0:T(8,128)(2,1)}, u32[]{:S(2)}) %copy-start.5) | copy-done | bytes 524312
  7.0 1.0 %copy-done.6 = bf16[2,256,512]{2,1,0:T(8,128)(2,1)S(1)} copy-done((bf16[2,256,512]{2,1,0:T(8,128)(2,1)S(1)}, bf16[2,256,512]{2,1,0:T(8,128)(2,1)}, u32[]{:S(2)}) %copy-start.6) | copy-done | bytes 524312
  8.1 0.9 %copy-done.7 = bf16[2,256,256]{2,1,0:T(8,128)(2,1)S(1)} copy-done((bf16[2,256,256]{2,1,0:T(8,128)(2,1)S(1)}, bf16[2,256,256]{2,1,0:T(8,128)(2,1)}, u32[]{:S(2)}) %copy-start.7) | copy-done | bytes 262168
  9.0 0.9 %copy-done.8 = bf16[2,256,256]{2,1,0:T(8,128)(2,1)S(1)} copy-done((bf16[2,256,256]{2,1,0:T(8,128)(2,1)S(1)}, bf16[2,256,256]{2,1,0:T(8,128)(2,1)}, u32[]{:S(2)}) %copy-start.8) | copy-done | bytes 262168
  10.0 0.7 copy-done.9
  10.7 0.7 copy-done.10
  11.3 55.6 %shard_map.173 = (bf16[20,128,128]{2,1,0:T(8,128)(2,1)S(1)}, bf16[20,128,128]{2,1,0:T(8,128)(2,1)S(1)}, f32[32,25600]{1,0:T(8,128)}, f32[8,128]{1,0:T(8,128)S(1)}) custom-call(bf16[20,128,128]{2,1,0:T(8,128)(2,1)S(1)} %bitcast.12, bf16[20,128,128]{2,1,0:T(8,128)(2,1)S(1)} %bitcast.13, bf16[32,25600]{1,0:T(8,128)(2,1)} %w.1, f32[20,20]{1,0:T(8,128)S(1)} %copy-done.9, ...), custom_call_target="tpu_custom_call" | custom-call | tf_op jit(solution)/shard_map/pallas_call | solution.py:486
  66.9 0.1 reshape.33
  67.0 0.0 copy-start.11
  67.0 0.5 slice_bitcast_fusion.1
  67.5 0.8 %copy.22 = bf16[20,32,4,128]{3,2,1,0:T(4,128)(2,1)} copy(bf16[20,32,4,128]{3,2,1,0:T(4,128)(2,1)S(1)} %bitcast.11) | data formatting | bytes 1310720
  68.4 0.8 %copy.23 = bf16[20,32,4,128]{3,2,1,0:T(4,128)(2,1)} copy(bf16[20,32,4,128]{3,2,1,0:T(4,128)(2,1)S(1)} %bitcast.10) | data formatting | bytes 1310720
  69.2 3.8 %copy.24 = f32[32,25600]{1,0:T(8,128)} copy(f32[32,25600]{1,0:T(8,128)} %get-tuple-element.20) | data formatting | bytes 6553600
  73.0 0.0 copy-done.11
  (7 shorter events, 0.0 us)
Async XLA Ops:
  0.6 1.2 %copy-start = (bf16[2,1024,256]{2,1,0:T(8,128)(2,1)S(1)}, bf16[2,1024,256]{2,1,0:T(8,128)(2,1)}, u32[]{:S(2)}) copy-start(bf16[2,1024,256]{2,1,0:T(8,128)(2,1)} %constant.16.clone.z8) | copy-start | bytes 3145732
  1.9 1.1 %copy-start.1 = (bf16[20,32,4,128]{3,2,1,0:T(4,128)(2,1)S(1)}, bf16[20,32,4,128]{3,2,1,0:T(4,128)(2,1)}, u32[]{:S(2)}) copy-start(bf16[20,32,4,128]{3,2,1,0:T(4,128)(2,1)} %param.14) | copy-start | bytes 1966084
  2.9 1.1 %copy-start.2 = (bf16[20,32,4,128]{3,2,1,0:T(4,128)(2,1)S(1)}, bf16[20,32,4,128]{3,2,1,0:T(4,128)(2,1)}, u32[]{:S(2)}) copy-start(bf16[20,32,4,128]{3,2,1,0:T(4,128)(2,1)} %param.15) | copy-start | bytes 1966084
  4.0 0.9 %copy-start.3 = (bf16[2,128,256]{2,1,0:T(8,128)(2,1)S(1)}, bf16[2,128,256]{2,1,0:T(8,128)(2,1)}, u32[]{:S(2)}) copy-start(bf16[2,128,256]{2,1,0:T(8,128)(2,1)} %constant.20.clone.ty.tyr) | copy-start | bytes 393220
  4.9 1.0 %copy-start.4 = (bf16[2,512,256]{2,1,0:T(8,128)(2,1)S(1)}, bf16[2,512,256]{2,1,0:T(8,128)(2,1)}, u32[]{:S(2)}) copy-start(bf16[2,512,256]{2,1,0:T(8,128)(2,1)} %constant.17.clone.z4) | copy-start | bytes 1572868
  6.0 1.0 %copy-start.5 = (bf16[2,512,256]{2,1,0:T(8,128)(2,1)S(1)}, bf16[2,512,256]{2,1,0:T(8,128)(2,1)}, u32[]{:S(2)}) copy-start(bf16[2,512,256]{2,1,0:T(8,128)(2,1)} %constant.21.clone.tyi) | copy-start | bytes 1572868
  7.0 1.0 %copy-start.6 = (bf16[2,256,512]{2,1,0:T(8,128)(2,1)S(1)}, bf16[2,256,512]{2,1,0:T(8,128)(2,1)}, u32[]{:S(2)}) copy-start(bf16[2,256,512]{2,1,0:T(8,128)(2,1)} %constant.23.clone.zi4) | copy-start | bytes 1572868
  8.1 0.9 %copy-start.7 = (bf16[2,256,256]{2,1,0:T(8,128)(2,1)S(1)}, bf16[2,256,256]{2,1,0:T(8,128)(2,1)}, u32[]{:S(2)}) copy-start(bf16[2,256,256]{2,1,0:T(8,128)(2,1)} %constant.18.clone.wx) | copy-start | bytes 786436
  9.0 0.9 %copy-start.8 = (bf16[2,256,256]{2,1,0:T(8,128)(2,1)S(1)}, bf16[2,256,256]{2,1,0:T(8,128)(2,1)}, u32[]{:S(2)}) copy-start(bf16[2,256,256]{2,1,0:T(8,128)(2,1)} %constant.19.clone.wxi) | copy-start | bytes 786436
  10.0 0.7 copy-start.9
  10.7 0.7 copy-start.10
  67.0 6.0 %copy-start.11 = (f32[21,24]{1,0:T(8,128)}, f32[21,24]{1,0:T(8,128)S(1)}, u32[]{:S(2)}) copy-start(f32[21,24]{1,0:T(8,128)S(1)} %reshape.33) | copy-start | bytes 6052
where the time goes:
time: 73.6 us; the launch traced here: 73 us
  Pallas kernels  55.6 us (76%)
  local copies, waits for them, and re-layouts  16.8 us (23%)
    pallas_call x1, Pallas kernels, per_device(): pl.pallas_call(partial(block_kernel, scale_fwd, scale_inv), out_shape=(ja...  55.6 us
    unnamed x27, local copies, waits for them, and re-layouts  16.2 us

commit v1 on v0

--- a/solution.py
+++ b/solution.py
@@ -119,6 +119,10 @@
 
 
 SLABS = 16
+TABLES = {}
+for name, rows in (("z8", 1024), ("wx", 256), ("z4", 512), ("ty", 128), ("tyi", 512),
+                   ("wxi", 256), ("zi8", 1024), ("zi4", 512), ("tyr", 128)):
+    TABLES[name] = (sum(count for _, count in TABLES.values()), rows)
 ROWS = 4
 F32 = jnp.float32
 BF16 = jnp.bfloat16
@@ -161,7 +165,9 @@
     zi8 = np.einsum("ab,rzk->rakbz", np.eye(8), fz).reshape(256, 8 * width_z)
     pick = np.stack([np.ones(1), np.zeros(1)]).reshape(2)
     zi4 = np.einsum("ab,rzk,e->raekbz", np.eye(4), fz, pick).reshape(256, 4 * width_z)
-    return [split_table(t) for t in (z8, z4, wx, wxi, ty, tyi, tyr, zi8, zi4)]
+    zi8 = np.concatenate(np.split(zi8, 4, axis=1))
+    zi4 = np.concatenate(np.split(zi4, 2, axis=1))
+    return split_table(np.concatenate([z8, wx, z4, ty, tyi, wxi, zi8, zi4, tyr]))
 
 
 def halves(value):
@@ -181,15 +187,20 @@
     return total
 
 
-def block_kernel(scale_fwd, scale_inv, sig, cot, w, mix, bias, z8, z4, wx, wxi, ty, tyi, tyr, zi8,
-                 zi4, act, gin, gspec, gsum, sf, point, dpre, modes, dmodes, spec, dspec, gmix,
-                 send, recv, sums, send_sem, recv_sem, sum_send, sum_recv):
+def block_kernel(scale_fwd, scale_inv, *refs):
+    sources, refs = refs[:4], refs[4:]
+    mix, bias, act, gin, gspec, gsum, sf, point, dpre, modes, dmodes, spec, dspec, gmix = refs[:14]
+    send, recv, sums, send_sem, recv_sem, sum_send, sum_recv, load_sem = refs[14:22]
+    places = refs[22:]
+    sig, tables, w, cot = places
+
+    def table(name, first=0, count=None):
+        start, rows = TABLES[name]
+        rows = slice(start + first, start + first + (count or rows))
+        return tables[0, rows], tables[1, rows]
     me = lax.axis_index("yslab")
     channels = 20
     lane = lax.broadcasted_iota(jnp.int32, (128, 128), 1)
-
-    def both(ref):
-        return ref[0], ref[1]
 
     def copy(step, chunk, peer):
         first, count = CHUNKS[chunk]
@@ -225,7 +236,8 @@
 
     def each_peer(action):
         def body(i, carry):
-            action(lax.rem(me + i, SLABS))
+            shift = 8 + lax.div(i, 2) * (1 - 2 * lax.rem(i, 2))
+            action(lax.rem(me + shift, SLABS))
             return carry
 
         lax.fori_loop(1, SLABS, body, 0)
@@ -239,16 +251,15 @@
         each_peer(lambda peer: arrival(step, chunk, peer).wait_recv())
 
     def forward_group(step, group, read, exact):
-        table = z8 if group < 2 else z4
+        name = "z8" if group < 2 else "z4"
         total = None
         for at in range(0, len(CHANS[group]), 2):
             pair = jnp.concatenate([read(c) for c in CHANS[group][at:at + 2]], axis=1)
             left = (pair, None) if exact else halves(pair)
-            rows = slice(at * 128, at * 128 + 256)
-            part = product(left, (table[0, rows], table[1, rows]))
+            part = product(left, table(name, at * 128, 256))
             total = part if total is None else total + part
         stacked = jnp.concatenate([total[:, :128], total[:, 128:]], axis=0)
-        out = product(both(wx), halves(stacked))
+        out = product(table("wx"), halves(stacked))
         if group < 2:
             for jl in range(2):
                 send[step, :, 2 * group + jl] = out[jl * 128:(jl + 1) * 128].reshape(16, 8, 128)
@@ -259,7 +270,7 @@
     def spectra(step, group, target, scale):
         for jl in range(2 if group < 2 else 1):
             tile = recv[step, :, 2 * group + jl].reshape(128, 128) * scale
-            out = product(halves(tile.T), both(ty))
+            out = product(halves(tile.T), table("ty"))
             if group < 2:
                 for place, c in enumerate(CHANS[group]):
                     target[jl, c] = out[place * 16:(place + 1) * 16]
@@ -278,12 +289,11 @@
         else:
             top = recv[step, :, 4].reshape(128, 128)
             low = pltpu.roll(top, 112, 1)
-        out = product(both(wxi), halves(jnp.concatenate([top, low], axis=0)))
+        out = product(table("wxi"), halves(jnp.concatenate([top, low], axis=0)))
         left = halves(jnp.concatenate([out[:128], out[128:]], axis=1))
-        table = zi8 if group < 2 else zi4
+        name = "zi8" if group < 2 else "zi4"
         for at in range(0, len(CHANS[group]), 2):
-            cols = slice(at * 128, at * 128 + 256)
-            field = product(left, (table[0, :, cols], table[1, :, cols]))
+            field = product(left, table(name, at * 128, 256))
             use(CHANS[group][at], field[:, :128])
             use(CHANS[group][at + 1], field[:, 128:])
 
@@ -302,6 +312,25 @@
 
         lax.fori_loop(0, 20, block, 0)
 
+    def rows_of(first, last):
+        return pl.ds(TABLES[first][0], TABLES[last][0] + TABLES[last][1] - TABLES[first][0])
+
+    early, late = rows_of("z8", "z4"), rows_of("ty", "tyr")
+
+    def load(index):
+        source, place = sources[index % 4], places[index % 4]
+        if index in (1, 5):
+            rows = early if index == 1 else late
+            source, place = source.at[:, rows], place.at[:, rows]
+        return pltpu.make_async_copy(source, place, load_sem.at[index])
+
+    def loaded(*indices):
+        for index in indices:
+            load(index).wait()
+
+    for index in (0, 1, 2, 5, 3):
+        load(index).start()
+
     barrier = pltpu.get_barrier_semaphore()
 
     def greet(peer):
@@ -310,29 +339,38 @@
 
     each_peer(greet)
     pl.semaphore_wait(barrier, SLABS - 1)
+
+    loaded(0, 1)
 
     for group in range(3):
         forward_group(0, group, lambda c: sig[c], True)
     sf[...] = sig[...].astype(F32)
     pointwise(sf, lambda a, b: mix[b, a], lambda a: bias[a])
+    loaded(2, 5, 3)
+
+    mixed = [(jnp.zeros((16, 640), F32), jnp.zeros((16, 640), F32)) for jl in range(2)]
     for group in range(3):
         wait_chunk(0, group)
         spectra(0, group, modes, scale_fwd)
-
+        for jl in range(2):
+            rows = slice(jl * 16, jl * 16 + 16)
+
+            def add(n, total):
+                if group < 2:
+                    c = lax.rem(n, 4) * 4 + 2 * group + lax.div(n, 4)
+                else:
+                    c = 16 + n
+                real, imag = total
+                wr = w[rows, pl.ds(pl.multiple_of(c * 640, 128), 640)].astype(F32)
+                wi = w[rows, pl.ds(pl.multiple_of(c * 640 + 12800, 128), 640)].astype(F32)
+                value = modes[jl, c]
+                ur = jnp.concatenate([value[:, :128]] * 5, axis=1)
+                ui = jnp.concatenate([value[:, 128:]] * 5, axis=1)
+                return real + wr * ur - wi * ui, imag + wr * ui + wi * ur
+
+            mixed[jl] = lax.fori_loop(0, len(CHANS[group]), add, mixed[jl])
     for jl in range(2):
-        rows = slice(jl * 16, jl * 16 + 16)
-
-        def add(c, total):
-            real, imag = total
-            wr = w[rows, pl.ds(pl.multiple_of(c * 640, 128), 640)].astype(F32)
-            wi = w[rows, pl.ds(pl.multiple_of(c * 640 + 12800, 128), 640)].astype(F32)
-            value = modes[jl, c]
-            ur = jnp.concatenate([value[:, :128]] * 5, axis=1)
-            ui = jnp.concatenate([value[:, 128:]] * 5, axis=1)
-            return real + wr * ur - wi * ui, imag + wr * ui + wi * ur
-
-        zero = jnp.zeros((16, 640), F32)
-        real, imag = lax.fori_loop(0, channels, add, (zero, zero))
+        real, imag = mixed[jl]
         for oq in range(5):
             cols = slice(oq * 128, (oq + 1) * 128)
             if oq < 4:
@@ -342,14 +380,17 @@
             for row in starts:
                 spec[row:row + 16, :128] = real[:, cols]
                 spec[row:row + 16, 128:] = imag[:, cols]
-    grid = product(both(tyi), halves(spec[...] * scale_inv), ((1,), (1,)))
     last = jnp.zeros((128, 128), F32)
-    for i in range(4):
-        send[1, :, i] = grid[i * 128:(i + 1) * 128, :128].reshape(16, 8, 128)
-        last = jnp.where(lane // 32 == i, grid[i * 128:(i + 1) * 128, 128:], last)
+    right = halves(spec[...] * scale_inv)
+    for q in range(2):
+        grid = product(table("tyi", q * 256, 256), right, ((1,), (1,)))
+        for ii in range(2):
+            part = grid[ii * 128:(ii + 1) * 128]
+            send[1, :, 2 * q + ii] = part[:, :128].reshape(16, 8, 128)
+            last = jnp.where(lane // 32 == 2 * q + ii, part[:, 128:], last)
+        send_chunk(1, q)
     send[1, :, 4] = last.reshape(16, 8, 128)
-    for group in range(3):
-        send_chunk(1, group)
+    send_chunk(1, 2)
 
     def activate(o, field):
         value = field + point[o]
@@ -366,7 +407,6 @@
         back_group(1, group, activate)
         forward_group(2, group, lambda c: dpre[c], False)
 
-    pointwise(dpre, lambda a, b: mix[a, b], lambda a: 0.0)
 
     def reduce_rows(value):
         return jnp.sum(value, axis=0, keepdims=True)
@@ -381,11 +421,11 @@
     lax.fori_loop(0, channels, pair_sums, 0)
     for o in range(channels):
         gmix[channels, o:o + 1] = reduce_rows(dpre[o])
-    flat = jnp.concatenate([gmix[...].reshape(504, 128), jnp.zeros((8, 128), F32)], axis=0)
+    flat = gmix[...].reshape(768, 128)
     line = lax.broadcasted_iota(jnp.int32, (8, 128), 0)
     ones = jnp.ones((8, 128), BF16)
     packed = jnp.zeros((8, 128), F32)
-    for r in range(4):
+    for r in range(6):
         high, low = halves(flat[r * 128:(r + 1) * 128])
         value = product((ones, None), (high, low), ((1,), (1,)))
         packed = jnp.where(line == r, value, packed)
@@ -426,7 +466,7 @@
                     folded = folded + value[:, oq * 128:(oq + 1) * 128]
                 dspec[row:row + 16, ri * 128:ri * 128 + 128] = folded
     for t in range(5):
-        grid = product(both(tyr), halves(dspec[t * 128:(t + 1) * 128] * scale_fwd), ((1,), (1,)))
+        grid = product(table("tyr"), halves(dspec[t * 128:(t + 1) * 128] * scale_fwd), ((1,), (1,)))
         send[3, :, t] = grid.reshape(16, 8, 128)
         if t == 1 or t == 3 or t == 4:
             send_chunk(3, t // 2)
@@ -455,6 +495,7 @@
 
         lax.fori_loop(0, channels, outer, 0)
 
+    pointwise(dpre, lambda a, b: mix[a, b], lambda a: 0.0)
     each_peer(lambda peer: sum_copy(peer, peer).wait_recv())
     gsum[...] = jnp.sum(sums[...], axis=0)
 
@@ -469,6 +510,21 @@
     for step in range(4):
         for group in range(3):
             each_peer(lambda peer: copy(step, group, peer).wait_send())
+
+
+def write_kernel(*refs):
+    sums, sources = refs[0], refs[1:4]
+    outs, gmix, gbias, sems = refs[4:7], refs[7], refs[8], refs[9]
+    copies = [pltpu.make_async_copy(sources[i], outs[i], sems.at[i]) for i in range(3)]
+    for copy in copies:
+        copy.start()
+    packed = sums[...]
+    for c in range(20):
+        at = (c % 4) * 32
+        gmix[c:c + 1, :] = packed[c // 4:c // 4 + 1, at:at + 20]
+    gbias[...] = packed[5:6, :20]
+    for copy in copies:
+        copy.wait()
 
 
 def per_device(signal, cotangent, spectral_weight, mix_weight, mix_bias):
@@ -479,19 +535,18 @@
     length_y = rows_y * slabs
     scale_fwd = 1.0 / math.sqrt(width_x * length_y * width_z)
     scale_inv = 1.0 / math.sqrt(4 * MODES**3)
-    tables_in = [jnp.asarray(t) for t in host_tables(width_x, length_y, width_z)]
     flat = (channels, width_x * rows_y, width_z)
+    packed = jnp.asarray(host_tables(width_x, length_y, width_z))
+    sources = [signal.reshape(flat), packed, spectral_weight, cotangent.reshape(flat)]
     vmem = pl.BlockSpec(memory_space=pltpu.VMEM)
     smem = pl.BlockSpec(memory_space=pltpu.SMEM)
+    hbm = pl.BlockSpec(memory_space=pltpu.HBM)
+    wide = jax.ShapeDtypeStruct(spectral_weight.shape, F32)
+    grid = jax.ShapeDtypeStruct(flat, BF16)
     act, gin, gspec, gsum = pl.pallas_call(
         partial(block_kernel, scale_fwd, scale_inv),
-        out_shape=(
-            jax.ShapeDtypeStruct(flat, BF16),
-            jax.ShapeDtypeStruct(flat, BF16),
-            jax.ShapeDtypeStruct(spectral_weight.shape, F32),
-            jax.ShapeDtypeStruct((8, 128), F32),
-        ),
-        in_specs=[vmem, vmem, vmem, smem, smem] + [vmem] * len(tables_in),
+        out_shape=(grid, grid, wide, jax.ShapeDtypeStruct((8, 128), F32)),
+        in_specs=[hbm] * 4 + [smem, smem],
         out_specs=(vmem, vmem, vmem, vmem),
         scratch_shapes=[
             pltpu.VMEM(flat, F32),
@@ -501,7 +556,7 @@
             pltpu.VMEM((2, 20, 16, 256), F32),
             pltpu.VMEM((256, 256), F32),
             pltpu.VMEM((640, 256), F32),
-            pltpu.VMEM((21, 24, 128), F32),
+            pltpu.VMEM((24, 32, 128), F32),
             pltpu.VMEM((4, SLABS, 5, 8, 128), F32),
             pltpu.VMEM((4, SLABS, 5, 8, 128), F32),
             pltpu.VMEM((SLABS, 8, 128), F32),
@@ -509,18 +564,23 @@
             pltpu.SemaphoreType.DMA((4, 3, SLABS)),
             pltpu.SemaphoreType.DMA((SLABS,)),
             pltpu.SemaphoreType.DMA((SLABS,)),
-        ],
+            pltpu.SemaphoreType.DMA((6,)),
+        ] + [pltpu.VMEM(x.shape, x.dtype) for x in sources],
         compiler_params=pltpu.CompilerParams(
-            collective_id=0, has_side_effects=True, vmem_limit_bytes=48 * 1024 * 1024
+            collective_id=0, has_side_effects=True, vmem_limit_bytes=30 * 1024 * 1024
         ),
-    )(
-        signal.reshape(flat), cotangent.reshape(flat), spectral_weight, mix_weight, mix_bias,
-        *tables_in,
-    )
-    full = gsum[:4].reshape(512)[:504].reshape(21, 24)
-    return (
-        act.reshape(signal.shape), gin.reshape(signal.shape), gspec, full[:20, :20], full[20, :20],
-    )
+    )(*sources, mix_weight, mix_bias)
+    act, gin, gspec, gmix, gbias = pl.pallas_call(
+        write_kernel,
+        out_shape=(
+            grid, grid, wide,
+            jax.ShapeDtypeStruct((20, 20), F32), jax.ShapeDtypeStruct((1, 20), F32),
+        ),
+        in_specs=[vmem] * 4,
+        out_specs=(hbm, hbm, hbm, vmem, vmem),
+        scratch_shapes=[pltpu.SemaphoreType.DMA((3,))],
+    )(gsum, act, gin, gspec)
+    return act.reshape(signal.shape), gin.reshape(signal.shape), gspec, gmix, gbias.reshape(20)
 
 
 def solution(mesh):

time: 73.6 us -> 71.4 us (0.970)
  local copies, waits for them, and re-layouts: 16.8 us -> 11.2 us
  Pallas kernels: 55.6 us -> 59.2 us
    unnamed x27 -> x20, local copies, waits for them, and re-layouts: 16.2 us -> 11.2 us
    pallas_call x1 -> x2, Pallas kernels: 55.6 us -> 59.2 us  [the longest x1 54.1 us: per_device(): pl.pallas_call(partial(block_kernel, scale_fwd, scale_inv), out_shape=(gr...]
where the time goes in v1:
time: 71.4 us; the launch traced here: 71 us
  Pallas kernels  59.2 us (83%)
  local copies, waits for them, and re-layouts  11.2 us (16%)
    pallas_call x1, Pallas kernels, per_device(): pl.pallas_call(partial(block_kernel, scale_fwd, scale_inv), out_shape=(gr...  54.1 us
    unnamed x20, local copies, waits for them, and re-layouts  11.2 us
    pallas_call x1, Pallas kernels, per_device(): pl.pallas_call(write_kernel, out_shape=(grid, grid, wide, jax.ShapeDtypeS...  5.1 us

profile of v1, /device:TPU:0, one launch (start us, length us, event | category | flops | bytes accessed | tf_op | source)
XLA Modules:
  0.0 71.0 jit_solution(17912244898819685111)
XLA Ops:
  0.6 0.0 copy-start
  0.6 2.3 %copy-done = bf16[2,4352,256]{2,1,0:T(8,128)(2,1)S(1)} copy-done((bf16[2,4352,256]{2,1,0:T(8,128)(2,1)S(1)}, bf16[2,4352,256]{2,1,0:T(8,128)(2,1)}, u32[]{:S(2)}) %copy-start) | copy-done | bytes 4456472
  2.9 0.0 copy-start.2
  2.9 1.4 %copy-done.2 = bf16[32,25600]{1,0:T(8,128)(2,1)S(1)} copy-done((bf16[32,25600]{1,0:T(8,128)(2,1)S(1)}, bf16[32,25600]{1,0:T(8,128)(2,1)}, u32[]{:S(2)}) %copy-start.2) | copy-done | bytes 1638424
  4.3 0.0 copy-start.3
  4.3 1.1 %copy-done.3 = bf16[20,32,4,128]{3,2,1,0:T(4,128)(2,1)S(1)} copy-done((bf16[20,32,4,128]{3,2,1,0:T(4,128)(2,1)S(1)}, bf16[20,32,4,128]{3,2,1,0:T(4,128)(2,1)}, u32[]{:S(2)}) %copy-start.3) | copy-done | bytes 655384
  5.4 0.0 copy-start.4
  5.4 1.1 %copy-done.4 = bf16[20,32,4,128]{3,2,1,0:T(4,128)(2,1)S(1)} copy-done((bf16[20,32,4,128]{3,2,1,0:T(4,128)(2,1)S(1)}, bf16[20,32,4,128]{3,2,1,0:T(4,128)(2,1)}, u32[]{:S(2)}) %copy-start.4) | copy-done | bytes 655384
  6.5 0.0 copy-start.7
  6.5 0.7 copy-done.7
  7.2 0.0 copy-start.9
  7.2 0.7 copy-done.9
  7.9 54.1 %shard_map.101 = (bf16[20,128,128]{2,1,0:T(8,128)(2,1)S(1)}, bf16[20,128,128]{2,1,0:T(8,128)(2,1)S(1)}, f32[32,25600]{1,0:T(8,128)S(1)}, f32[8,128]{1,0:T(8,128)S(1)}) custom-call(bf16[20,128,128]{2,1,0:T(8,128)(2,1)S(1)} %bitcast.5, bf16[2,4352,256]{2,1,0:T(8,128)(2,1)S(1)} %copy-done, bf16[32,25600]{1,0:T(8,128)(2,1)S(1)} %copy-done.2, ...), custom_call_target="tpu_custom_call" | custom-call | tf_op jit(solution)/shard_map/pallas_call | solution.py:546
  62.0 0.0 copy-start.1
  62.0 1.7 %copy-done.1 = f32[32,25600]{1,0:T(8,128)} copy-done((f32[32,25600]{1,0:T(8,128)}, f32[32,25600]{1,0:T(8,128)S(1)}, u32[]{:S(2)}) %copy-start.1) | copy-done | bytes 3276824
  63.7 0.0 copy-start.5
  63.7 0.8 %copy-done.5 = bf16[20,128,128]{2,1,0:T(8,128)(2,1)} copy-done((bf16[20,128,128]{2,1,0:T(8,128)(2,1)}, bf16[20,128,128]{2,1,0:T(8,128)(2,1)S(1)}, u32[]{:S(2)}) %copy-start.5) | copy-done | bytes 655384
  64.5 0.0 copy-start.6
  64.5 0.8 %copy-done.6 = bf16[20,128,128]{2,1,0:T(8,128)(2,1)} copy-done((bf16[20,128,128]{2,1,0:T(8,128)(2,1)}, bf16[20,128,128]{2,1,0:T(8,128)(2,1)S(1)}, u32[]{:S(2)}) %copy-start.6) | copy-done | bytes 655384
  65.4 0.0 copy-start.8
  65.4 0.6 copy-done.8
  65.9 5.1 %shard_map.102 = (bf16[20,128,128]{2,1,0:T(8,128)(2,1)}, bf16[20,128,128]{2,1,0:T(8,128)(2,1)}, f32[32,25600]{1,0:T(8,128)}, f32[20,20]{1,0:T(8,128)}, f32[1,20]{1,0:T(1,128)}) custom-call(f32[8,128]{1,0:T(8,128)} %copy-done.8, bf16[20,128,128]{2,1,0:T(8,128)(2,1)} %copy-done.5, bf16[20,128,128]{2,1,0:T(8,128)(2,1)} %copy-done.6, f32[32,25600]{1,0:T(8,128)} %copy-done.1), custom_call_target="tpu_custom_call" | custom-call | tf_op jit(solution)/shard_map/pallas_call | solution.py:573
Async XLA Ops:
  0.6 2.3 %copy-start = (bf16[2,4352,256]{2,1,0:T(8,128)(2,1)S(1)}, bf16[2,4352,256]{2,1,0:T(8,128)(2,1)}, u32[]{:S(2)}) copy-start(bf16[2,4352,256]{2,1,0:T(8,128)(2,1)} %constant.2.clone.refs_1_) | copy-start | bytes 13369348
  2.9 1.4 %copy-start.2 = (bf16[32,25600]{1,0:T(8,128)(2,1)S(1)}, bf16[32,25600]{1,0:T(8,128)(2,1)}, u32[]{:S(2)}) copy-start(bf16[32,25600]{1,0:T(8,128)(2,1)} %refs_2_.1) | copy-start | bytes 4915204
  4.3 1.1 %copy-start.3 = (bf16[20,32,4,128]{3,2,1,0:T(4,128)(2,1)S(1)}, bf16[20,32,4,128]{3,2,1,0:T(4,128)(2,1)}, u32[]{:S(2)}) copy-start(bf16[20,32,4,128]{3,2,1,0:T(4,128)(2,1)} %param.6) | copy-start | bytes 1966084
  5.4 1.1 %copy-start.4 = (bf16[20,32,4,128]{3,2,1,0:T(4,128)(2,1)S(1)}, bf16[20,32,4,128]{3,2,1,0:T(4,128)(2,1)}, u32[]{:S(2)}) copy-start(bf16[20,32,4,128]{3,2,1,0:T(4,128)(2,1)} %param.7) | copy-start | bytes 1966084
  6.5 0.7 copy-start.7
  7.2 0.7 copy-start.9
  62.0 1.7 %copy-start.1 = (f32[32,25600]{1,0:T(8,128)}, f32[32,25600]{1,0:T(8,128)S(1)}, u32[]{:S(2)}) copy-start(f32[32,25600]{1,0:T(8,128)S(1)} %get-tuple-element.17.refs_3_) | copy-start | bytes 9830404
  63.7 0.8 %copy-start.5 = (bf16[20,128,128]{2,1,0:T(8,128)(2,1)}, bf16[20,128,128]{2,1,0:T(8,128)(2,1)S(1)}, u32[]{:S(2)}) copy-start(bf16[20,128,128]{2,1,0:T(8,128)(2,1)S(1)} %get-tuple-element.15.refs_1_) | copy-start | bytes 1966084
  64.5 0.8 %copy-start.6 = (bf16[20,128,128]{2,1,0:T(8,128)(2,1)}, bf16[20,128,128]{2,1,0:T(8,128)(2,1)S(1)}, u32[]{:S(2)}) copy-start(bf16[20,128,128]{2,1,0:T(8,128)(2,1)S(1)} %get-tuple-element.16.refs_2_) | copy-start | bytes 1966084
  65.4 0.6 copy-start.8

commit v2 on v1

--- a/solution.py
+++ b/solution.py
@@ -579,6 +579,7 @@
         in_specs=[vmem] * 4,
         out_specs=(hbm, hbm, hbm, vmem, vmem),
         scratch_shapes=[pltpu.SemaphoreType.DMA((3,))],
+        compiler_params=pltpu.CompilerParams(vmem_limit_bytes=4 * 1024 * 1024),
     )(gsum, act, gin, gspec)
     return act.reshape(signal.shape), gin.reshape(signal.shape), gspec, gmix, gbias.reshape(20)
 

time: 71.4 us -> 65.1 us (0.912)
  local copies, waits for them, and re-layouts: 11.2 us -> 7.22 us
  Pallas kernels: 59.2 us -> 56.9 us
    unnamed x20 -> x12, local copies, waits for them, and re-layouts: 11.2 us -> 7.22 us
    pallas_call x1, Pallas kernels: 5.1 us -> 2.77 us  [per_device(): pl.pallas_call(write_kernel, out_shape=(grid, grid, wide, jax.ShapeDtypeS...]
where the time goes in v2:
time: 65.1 us; the launch traced here: 64.7 us
  Pallas kernels  56.9 us (87%)
  local copies, waits for them, and re-layouts  7.22 us (11%)
    pallas_call x1, Pallas kernels, per_device(): pl.pallas_call(partial(block_kernel, scale_fwd, scale_inv), out_shape=(gr...  54.1 us
    unnamed x12, local copies, waits for them, and re-layouts  7.22 us
    pallas_call x1, Pallas kernels, per_device(): pl.pallas_call(write_kernel, out_shape=(grid, grid, wide, jax.ShapeDtypeS...  2.77 us

profile of v2, /device:TPU:0, one launch (start us, length us, event | category | flops | bytes accessed | tf_op | source)
XLA Modules:
  0.0 64.7 jit_solution(10868431006063154058)
XLA Ops:
  0.6 0.0 copy-start
  0.6 2.3 %copy-done = bf16[2,4352,256]{2,1,0:T(8,128)(2,1)S(1)} copy-done((bf16[2,4352,256]{2,1,0:T(8,128)(2,1)S(1)}, bf16[2,4352,256]{2,1,0:T(8,128)(2,1)}, u32[]{:S(2)}) %copy-start) | copy-done | bytes 4456472
  2.9 0.0 copy-start.1
  2.9 1.4 %copy-done.1 = bf16[32,25600]{1,0:T(8,128)(2,1)S(1)} copy-done((bf16[32,25600]{1,0:T(8,128)(2,1)S(1)}, bf16[32,25600]{1,0:T(8,128)(2,1)}, u32[]{:S(2)}) %copy-start.1) | copy-done | bytes 1638424
  4.3 0.0 copy-start.2
  4.3 1.1 %copy-done.2 = bf16[20,32,4,128]{3,2,1,0:T(4,128)(2,1)S(1)} copy-done((bf16[20,32,4,128]{3,2,1,0:T(4,128)(2,1)S(1)}, bf16[20,32,4,128]{3,2,1,0:T(4,128)(2,1)}, u32[]{:S(2)}) %copy-start.2) | copy-done | bytes 655384
  5.4 0.0 copy-start.3
  5.4 1.1 %copy-done.3 = bf16[20,32,4,128]{3,2,1,0:T(4,128)(2,1)S(1)} copy-done((bf16[20,32,4,128]{3,2,1,0:T(4,128)(2,1)S(1)}, bf16[20,32,4,128]{3,2,1,0:T(4,128)(2,1)}, u32[]{:S(2)}) %copy-start.3) | copy-done | bytes 655384
  6.5 0.0 copy-start.4
  6.5 0.7 %copy-done.4 = f32[20,20]{1,0:T(8,128)S(1)} copy-done((f32[20,20]{1,0:T(8,128)S(1)}, f32[20,20]{1,0:T(8,128)}, u32[]{:S(2)}) %copy-start.4) | copy-done | bytes 1624
  7.2 0.0 copy-start.5
  7.2 0.7 %copy-done.5 = f32[20]{0:T(128)S(1)} copy-done((f32[20]{0:T(128)S(1)}, f32[20]{0:T(128)}, u32[]{:S(2)}) %copy-start.5) | copy-done | bytes 104
  7.9 54.1 %shard_map.101 = (bf16[20,128,128]{2,1,0:T(8,128)(2,1)S(1)}, bf16[20,128,128]{2,1,0:T(8,128)(2,1)S(1)}, f32[32,25600]{1,0:T(8,128)S(1)}, f32[8,128]{1,0:T(8,128)S(1)}) custom-call(bf16[20,128,128]{2,1,0:T(8,128)(2,1)S(1)} %bitcast.5, bf16[2,4352,256]{2,1,0:T(8,128)(2,1)S(1)} %copy-done, bf16[32,25600]{1,0:T(8,128)(2,1)S(1)} %copy-done.1, ...), custom_call_target="tpu_custom_call" | custom-call | tf_op jit(solution)/shard_map/pallas_call | solution.py:546
  62.0 2.8 %shard_map.102 = (bf16[20,128,128]{2,1,0:T(8,128)(2,1)}, bf16[20,128,128]{2,1,0:T(8,128)(2,1)}, f32[32,25600]{1,0:T(8,128)}, f32[20,20]{1,0:T(8,128)}, f32[1,20]{1,0:T(1,128)}) custom-call(f32[8,128]{1,0:T(8,128)S(1)} %get-tuple-element.14.refs_0_, bf16[20,128,128]{2,1,0:T(8,128)(2,1)S(1)} %get-tuple-element.15.refs_1_, ...), custom_call_target="tpu_custom_call" | custom-call | tf_op jit(solution)/shard_map/pallas_call | solution.py:573
Async XLA Ops:
  0.6 2.3 %copy-start = (bf16[2,4352,256]{2,1,0:T(8,128)(2,1)S(1)}, bf16[2,4352,256]{2,1,0:T(8,128)(2,1)}, u32[]{:S(2)}) copy-start(bf16[2,4352,256]{2,1,0:T(8,128)(2,1)} %constant.2.clone.refs_1_) | copy-start | bytes 13369348
  2.9 1.4 %copy-start.1 = (bf16[32,25600]{1,0:T(8,128)(2,1)S(1)}, bf16[32,25600]{1,0:T(8,128)(2,1)}, u32[]{:S(2)}) copy-start(bf16[32,25600]{1,0:T(8,128)(2,1)} %refs_2_.1) | copy-start | bytes 4915204
  4.3 1.1 %copy-start.2 = (bf16[20,32,4,128]{3,2,1,0:T(4,128)(2,1)S(1)}, bf16[20,32,4,128]{3,2,1,0:T(4,128)(2,1)}, u32[]{:S(2)}) copy-start(bf16[20,32,4,128]{3,2,1,0:T(4,128)(2,1)} %param.6) | copy-start | bytes 1966084
  5.4 1.1 %copy-start.3 = (bf16[20,32,4,128]{3,2,1,0:T(4,128)(2,1)S(1)}, bf16[20,32,4,128]{3,2,1,0:T(4,128)(2,1)}, u32[]{:S(2)}) copy-start(bf16[20,32,4,128]{3,2,1,0:T(4,128)(2,1)} %param.7) | copy-start | bytes 1966084
  6.5 0.7 %copy-start.4 = (f32[20,20]{1,0:T(8,128)S(1)}, f32[20,20]{1,0:T(8,128)}, u32[]{:S(2)}) copy-start(f32[20,20]{1,0:T(8,128)} %refs_4_.1) | copy-start | bytes 4804
  7.2 0.7 %copy-start.5 = (f32[20]{0:T(128)S(1)}, f32[20]{0:T(128)}, u32[]{:S(2)}) copy-start(f32[20]{0:T(128)} %refs_5_.1) | copy-start | bytes 244
